TPU v7x, 32 devices: a whole 2x2x4 slice. The times are simulated.
32 devices in a mesh: seg: 4 (over y, core), term: 8 (over z, x).
Axes of the slice: x: 2, y: 2, z: 4, core: 2. Of those that a mesh axis runs over, the one named last changes fastest.
Arguments:
- envs_left: float32 [4, 16, 8, 128, 128], P('seg', 'term'), may hold values from -0.5 to 0.5
- envs_right: float32 [4, 16, 8, 128, 128], P('seg', 'term'), may hold values from -0.5 to 0.5
- site_left: float32 [4, 6, 128, 128], P('seg'), may hold values from -6 to 6
- site_right: float32 [4, 6, 128, 128], P('seg'), may hold values from -6 to 6
- precondition: float32 [4, 6, 16384], P('seg'), may hold values from 1 to 10
- source_block: int32 [4, 16, 6], P('seg', 'term'), may hold values from -1 to 5, as said below
- left_tile: int32 [4, 6], P('seg'), may hold values from 0 to 7
- right_tile: int32 [4, 6], P('seg'), may hold values from 0 to 7
Outputs:
- ground_vector: float32 [4, 6, 16384], P('seg', None, 'term')
- ground_energy: float32 [4], P('seg')
Inputs may be any that keep to these rules, and one draw needn't show every extreme that they name: `source_block`: -1 means that the term leaves the output block out; every term's non-negative entries are distinct blocks, and the number of blocks a term feeds varies from 1 to 6 over the terms.
All inputs are finite; a program needn't handle non-finite values.
Results may differ from a plain program's by a relative error of at most 0.0003.
Values sent between devices are 32-bit elements; how exact they have to be, the bound alone decides.
A program may use at most 64 MiB of HBM per device.

v0:
```python
import math

import jax
import jax.numpy as jnp
from jax import lax
from jax.sharding import PartitionSpec as P

ITERS = 4


FINEST = lax.Precision.HIGHEST
EPSILON = 1e-06


def passed_along(value, axis, steps):
    count = lax.axis_size(axis)
    pairs = [(source, (source + steps) % count) for source in range(count)]
    return lax.ppermute(value, axis, pairs)


def ritz_pair(energy, coupling, curvature):
    half_gap = 0.5 * (energy - curvature)
    radius = jnp.sqrt(half_gap * half_gap + coupling * coupling)
    lowest = 0.5 * (energy + curvature) - radius
    keep_coef = jnp.where(
        half_gap >= 0, coupling * coupling / (radius + jnp.abs(half_gap)), radius - half_gap
    )
    length = jnp.sqrt(keep_coef * keep_coef + coupling * coupling)
    return (lowest, keep_coef / length, -coupling / length)


def select_terms(left_envs, right_envs, sources, left_ids, right_ids):
    block_count = sources.shape[1]
    left_chosen = left_envs[:, left_ids]
    right_chosen = right_envs[:, right_ids]
    safe_sources = jnp.clip(sources, 0, block_count - 1)
    active_mask = (sources >= 0).astype(jnp.float32)[:, :, None, None]
    return (left_chosen, right_chosen, safe_sources, active_mask)


def local_terms(vector, selected):
    left_chosen, right_chosen, safe_sources, active_mask = selected
    block_count = safe_sources.shape[1]
    tile_edge = left_chosen.shape[-1]
    tile_stack = vector.reshape(block_count, tile_edge, tile_edge)
    pieces = tile_stack[safe_sources] * active_mask
    inner_prod = jnp.einsum("tkab,tkbc->tkac", left_chosen, pieces, precision=FINEST)
    outer_prod = jnp.einsum("tkac,tkdc->tkad", inner_prod, right_chosen, precision=FINEST)
    summed = jnp.sum(outer_prod, axis=0)
    return summed.reshape(block_count, tile_edge * tile_edge)


def shards(
    envs_left, envs_right, site_left, site_right, precondition, source_block, left_tile, right_tile
):
    envs_next, site_next = passed_along((envs_right, site_right), "seg", -1)
    selected = select_terms(
        envs_left[0], envs_next[0], source_block[0], left_tile[0], right_tile[0]
    )
    precond = precondition[0]
    block_count = site_left.shape[1]
    tile_edge = site_left.shape[2]
    full_width = tile_edge * tile_edge
    guess = jnp.einsum("kab,kbc->kac", site_left[0], site_next[0], precision=FINEST).reshape(
        block_count, full_width
    )
    vector = guess / jnp.sqrt(jnp.sum(guess * guess) + EPSILON)
    share_width = full_width // lax.axis_size("term")
    offset = lax.axis_index("term") * share_width

    def apply_local(full_vector):
        return local_terms(full_vector, selected)

    def apply_whole(full_vector):
        return lax.psum(apply_local(full_vector), "term")

    image = apply_whole(vector)
    for iteration in range(ITERS):
        energy = jnp.sum(vector * image)
        residual = image - energy * vector
        scaled = residual / precond
        projection = jnp.sum(vector * scaled)
        remainder = scaled - projection * vector
        search = remainder / jnp.sqrt(jnp.sum(remainder * remainder) + EPSILON)
        search_image = apply_whole(search)
        coupling = 0.5 * (jnp.sum(vector * search_image) + jnp.sum(search * image))
        curvature = jnp.sum(search * search_image)
        lowest, keep_coef, mix_coef = ritz_pair(energy, coupling, curvature)
        vector = keep_coef * vector + mix_coef * search
        image = keep_coef * image + mix_coef * search_image
    energy = jnp.sum(vector * image)
    mine = lax.dynamic_slice_in_dim(vector, offset, share_width, 1)
    scale_factor = math.sqrt(block_count * full_width)
    return ((mine * scale_factor)[None], jnp.reshape(energy, (1,)))


def solution(mesh):
    in_specs = (
        P("seg", "term", None, None, None),
        P("seg", "term", None, None, None),
        P("seg", None, None, None),
        P("seg", None, None, None),
        P("seg", None, None),
        P("seg", "term", None),
        P("seg", None),
        P("seg", None),
    )
    out_specs = (P("seg", None, "term"), P("seg"))
    return jax.shard_map(shards, mesh=mesh, in_specs=in_specs, out_specs=out_specs, check_vma=False)
```

profile of v0, /device:TPU:0, one launch (start us, length us, event | category | flops | bytes accessed | tf_op | source)
XLA Modules:
  0.0 486.1 jit_solution(3211896871637686112)
XLA Ops:
  7.2 2.5 collective-permute-start
  9.7 0.7 collective-permute-start.1
  10.4 0.7 compare_select_fusion
  11.0 0.1 reshape.147
  11.1 0.6 copy-done.19
  11.8 0.6 copy-done.20
  12.5 0.6 gather_fusion
  13.2 2.1 collective-permute-done
  15.3 1.2 multiply_reduce_fusion.22
  17.2 1.5 gather_fusion.1
  18.7 3.0 fusion.11
  21.7 4.8 collective-permute-done.1
  26.5 1.8 gather_fusion.2
  28.4 2.0 convolution_bitcast_fusion.4
  30.4 1.1 copy.113
  31.6 74.1 %all-reduce.6.cloned.1.call-done = f32[6,16384]{1,0:T(8,128)} async-done(((f32[6,16384]{1,0:T(8,128)}), f32[6,16384]{1,0:T(8,128)}) %all-reduce.6.cloned.1.call-update) | async-done | bytes 393232 | tf_op jit(solution)/shard_map/psum | solution.py:75
  105.6 2.0 fusion.20
  107.6 1.7 fusion.23
  109.3 2.4 multiply_reduce_fusion.21
  112.5 2.8 broadcast_divide_fusion.3
  115.3 0.8 copy-done.15
  116.1 0.8 copy.117
  116.9 2.5 gather_fusion.3
  119.4 2.1 fusion.9
  121.5 0.9 convolution_bitcast_fusion.3
  122.4 1.1 copy.112
  123.5 71.8 %all-reduce.8.cloned.1.call-done = f32[6,16384]{1,0:T(8,128)} async-done(((f32[6,16384]{1,0:T(8,128)}), f32[6,16384]{1,0:T(8,128)}) %all-reduce.8.cloned.1.call-update) | async-done | bytes 393232 | tf_op jit(solution)/shard_map/psum | solution.py:75
  195.3 2.3 multiply_reduce_fusion.20
  200.4 2.3 multiply_reduce_fusion.18
  202.7 1.5 multiply_reduce_fusion.17
  204.2 2.3 multiply_reduce_fusion.16
  207.2 2.8 broadcast_divide_fusion.2
  210.0 0.8 copy-done.11
  210.9 1.5 gather_fusion.4
  212.3 2.1 fusion.7
  214.4 0.9 convolution_bitcast_fusion.2
  215.3 1.0 copy.111
  216.4 0.2 all-reduce.12.cloned.1.call-start
  216.6 71.6 %all-reduce.10.cloned.1.call-done = f32[6,16384]{1,0:T(8,128)} async-done(((f32[6,16384]{1,0:T(8,128)}), f32[6,16384]{1,0:T(8,128)}) %all-reduce.10.cloned.1.call-update) | async-done | bytes 393232 | tf_op jit(solution)/shard_map/psum | solution.py:75
  288.2 2.2 multiply_reduce_fusion.15
  293.2 2.1 multiply_reduce_fusion.12
  295.3 1.5 multiply_reduce_fusion.11
  296.8 2.3 multiply_reduce_fusion.10
  299.8 2.8 broadcast_divide_fusion.1
  302.6 0.8 copy-done.12
  303.5 1.5 gather_fusion.5
  305.0 2.1 fusion.5
  307.0 0.9 convolution_bitcast_fusion.1
  307.9 1.0 copy.110
  309.1 71.8 %all-reduce.12.cloned.1.call-done = f32[6,16384]{1,0:T(8,128)} async-done(((f32[6,16384]{1,0:T(8,128)}), f32[6,16384]{1,0:T(8,128)}) %all-reduce.12.cloned.1.call-update) | async-done | bytes 393232 | tf_op jit(solution)/shard_map/psum | solution.py:75
  380.8 2.2 multiply_reduce_fusion.9
  385.7 2.3 multiply_reduce_fusion.6
  388.0 1.5 multiply_reduce_fusion.5
  389.5 2.3 multiply_reduce_fusion.4
  392.5 2.6 broadcast_divide_fusion
  395.1 0.8 copy-done.13
  396.0 1.5 gather_fusion.6
  397.5 2.1 fusion.13
  399.6 0.9 convolution_bitcast_fusion
  400.5 1.1 copy.109
  401.6 71.8 %all-reduce.14.cloned.1.call-done = f32[6,16384]{1,0:T(8,128)} async-done(((f32[6,16384]{1,0:T(8,128)}), f32[6,16384]{1,0:T(8,128)}) %all-reduce.14.cloned.1.call-update) | async-done | bytes 393232 | tf_op jit(solution)/shard_map/psum | solution.py:75
  473.4 2.0 multiply_reduce_fusion.3
  478.1 0.8 multiply_reduce_fusion
  478.9 0.7 broadcast_in_dim.2
  (57 shorter events, 0.7 us)
Async XLA Ops:
  7.2 5.3 %copy-start = (f32[1,2,8,128,128]{4,3,2,1,0:T(8,128)S(1)}, f32[1,2,8,128,128]{4,3,2,1,0:T(8,128)}, u32[]{:S(2)}) copy-start(f32[1,2,8,128,128]{4,3,2,1,0:T(8,128)} %param.8) | copy-start | bytes 3145732
  7.2 98.4 %all-reduce.6.cloned.1.call-start = ((), (), s32[]{:S(2)}) async-start(), calls=%async_computation | async-start | bytes 1048576 | tf_op jit(solution)/shard_map/psum | solution.py:75
  7.2 8.1 %collective-permute-start = (f32[1,6,128,128]{3,2,1,0:T(8,128)}, f32[1,6,128,128]{3,2,1,0:T(8,128)S(1)}, u32[]{:S(2)}, u32[]{:S(2)}) collective-permute-start(f32[1,6,128,128]{3,2,1,0:T(8,128)} %param.11), channel_id=1, source_target_pairs={{0,24},{8,0},{16,8},{24,16},{1,25},{9,1},{17,9},{25,17},{2,26},{10... | collective-permute-start | bytes 1179656 | tf_op jit(solution)/shard_map/ppermute | solution.py:18
  9.7 16.8 %collective-permute-start.1 = (f32[1,2,8,128,128]{4,3,2,1,0:T(8,128)}, f32[1,2,8,128,128]{4,3,2,1,0:T(8,128)}, u32[]{:S(2)}, u32[]{:S(2)}) collective-permute-start(f32[1,2,8,128,128]{4,3,2,1,0:T(8,128)} %param.9), channel_id=1, source_target_pairs={{0,24},{8,0},{16,8},{24,16},{1,25},{9,1},{17,9},{25,17},{2,26},{10... | collective-permute-start | bytes 3145736 | tf_op jit(solution)/shard_map/ppermute | solution.py:18
  11.1 0.7 copy-start.19
  11.8 0.7 copy-start.20
  12.5 0.7 copy-start.18
  12.5 2.8 copy-start.17
  31.4 163.8 %all-reduce.8.cloned.1.call-start = ((), (), s32[]{:S(2)}) async-start(), calls=%async_computation.1 | async-start | bytes 1048576 | tf_op jit(solution)/shard_map/psum | solution.py:75
  31.5 76.0 %copy-start.1 = (f32[1,6,16384]{2,0,1:T(1,128)S(1)}, f32[1,6,16384]{2,0,1:T(1,128)}, u32[]{:S(2)}) copy-start(f32[1,6,16384]{2,0,1:T(1,128)} %param.12) | copy-start | bytes 1179652
  105.6 2.0 copy-start.10
  115.3 0.8 copy-start.15
  123.4 164.8 %all-reduce.10.cloned.1.call-start = ((), (), s32[]{:S(2)}) async-start(), calls=%async_computation.2 | async-start | bytes 1048576 | tf_op jit(solution)/shard_map/psum | solution.py:75
  202.7 1.5 copy-start.4
  202.7 1.5 copy-start.6
  210.0 0.8 copy-start.11
  215.3 72.9 %copy-start.5 = (f32[6,16384]{1,0:T(8,128)S(1)}, f32[6,16384]{1,0:T(8,128)}, u32[]{:S(2)}) copy-start(f32[6,16384]{1,0:T(8,128)} %copy-done.4) | copy-start | bytes 1179652
  216.4 164.5 %all-reduce.12.cloned.1.call-start = ((), (), s32[]{:S(2)}) async-start(), calls=%async_computation.3 | async-start | bytes 1048576 | tf_op jit(solution)/shard_map/psum | solution.py:75
  295.3 1.5 copy-start.7
  295.3 1.5 copy-start.9
  302.6 0.8 copy-start.12
  307.9 72.9 %copy-start.8 = (f32[6,16384]{1,0:T(8,128)S(1)}, f32[6,16384]{1,0:T(8,128)}, u32[]{:S(2)}) copy-start(f32[6,16384]{1,0:T(8,128)} %copy-done.7) | copy-start | bytes 1179652
  309.0 164.4 %all-reduce.14.cloned.1.call-start = ((), (), s32[]{:S(2)}) async-start(), calls=%async_computation.4 | async-start | bytes 1048576 | tf_op jit(solution)/shard_map/psum | solution.py:75
  388.0 1.5 copy-start.2
  395.1 0.8 copy-start.13
  400.5 72.9 %copy-start.3 = (f32[6,16384]{1,0:T(8,128)S(1)}, f32[6,16384]{1,0:T(8,128)}, u32[]{:S(2)}) copy-start(f32[6,16384]{1,0:T(8,128)} %copy-done.2) | copy-start | bytes 1179652
  400.5 72.9 %copy-start.14 = (f32[6,16384]{1,0:T(8,128)S(1)}, f32[6,16384]{1,0:T(8,128)}, u32[]{:S(2)}) copy-start(f32[6,16384]{1,0:T(8,128)} %copy-done.13) | copy-start | bytes 1179652
  473.4 4.7 copy-start.16
Sparse Core Ops, SparseCore 0:
  31.6 73.9 all-reduce.5
  123.6 71.6 all-reduce.7
  216.5 71.6 all-reduce.9
  309.1 71.6 all-reduce.11
  401.7 71.6 all-reduce.13
where the time goes:
time: 487 us; the launch traced here: 486 us
  waiting for transfers between devices  368 us (76%)
  other arithmetic  45.3 us (9%)
  between operations  28.7 us (6%)
  local copies, waits for them, and re-layouts  22.5 us (5%)
  matrix products  18 us (4%)
    psum x5, waiting for transfers between devices, apply_whole(): return lax.psum(apply_local(full_vector), 'term')  361 us
    dot_general x5, matrix products, local_terms(): jnp.einsum('tkab,tkbc->tkac', left_chosen, pieces, precision=FINEST)  11.3 us
    div x4, other arithmetic, shards(): search = remainder / jnp.sqrt(jnp.sum(remainder * remainder) + EPSILON)  11 us
    unnamed x51, local copies, waits for them, and re-layouts  10.9 us
  transfers between devices with their start and end apart: 7, of which 7 were waited for; matrix products, arithmetic and copies ran while one was open for 1% of the time, Pallas kernels for 0%

commit v1 on v0

v1 whole, which is shorter than its diff:
```python
import functools
import math

import jax
import jax.numpy as jnp
from jax import lax
from jax.experimental import pallas as pl
from jax.experimental.pallas import tpu as pltpu
from jax.sharding import PartitionSpec as P

ITERS = 4
EPSILON = 1e-06
MESH = pl.DeviceIdType.MESH
F32 = jnp.float32
BF16 = jnp.bfloat16


def split(value):
    high = value.astype(BF16)
    low = (value - high.astype(F32)).astype(BF16)
    return high, low


def dot(a, b):
    return lax.dot_general(a, b, (((1,), (0,)), ((), ())), preferred_element_type=F32)


def total_of(value):
    return jnp.sum(jnp.sum(value, axis=0, keepdims=True), axis=1, keepdims=True)


def folded(value):
    return jnp.sum(value.reshape(value.shape[0] // 8, 8, value.shape[1]), axis=0)


def kernel(
    devices, segs, blocks, tile, terms, share,
    left_hbm, right_hbm, site_left_hbm, site_right_hbm, precond_hbm, sources, left_ids, right_ids,
    out_ref, energy_ref,
    left, right, site_left, site_right, precond, left_split, right_high, right_low,
    search_high, search_low, picked, feed_high, feed_low, inverse, search, vector, image, search_image, part, pair_in, line_out, line_in,
    local_sems, seg_send, seg_recv, pair_send, pair_recv, line_send, line_recv,
    out_send, out_recv, across_send, across_recv,
):
    me = lax.axis_index("term")
    seg = lax.axis_index("seg")
    column, place = me % 2, me // 2
    places = devices // 2
    partner = place * 2 + 1 - column
    before, after = (seg + segs - 1) % segs, (seg + 1) % segs
    piece = blocks * tile // devices

    def rows(owner):
        return pl.ds(pl.multiple_of(owner * piece, 8), piece)

    def peer(distance):
        return (place + distance) % places

    locals_ = [
        pltpu.make_async_copy(source, target, local_sems.at[n])
        for n, (source, target) in enumerate(
            [(site_left_hbm, site_left), (left_hbm, left), (precond_hbm, precond)]
        )
    ]
    for copy in locals_:
        copy.start()

    barrier = pltpu.get_barrier_semaphore()
    pl.semaphore_signal(barrier, inc=1, device_id={"seg": before}, device_id_type=MESH)
    pl.semaphore_signal(barrier, inc=1, device_id={"seg": after}, device_id_type=MESH)
    pl.semaphore_signal(barrier, inc=1, device_id={"term": partner}, device_id_type=MESH)
    for distance in range(1, places):
        pl.semaphore_signal(
            barrier, inc=1, device_id={"term": peer(distance) * 2 + column}, device_id_type=MESH
        )
    pl.semaphore_wait(barrier, places + 2)

    seg_copies = [
        pltpu.make_async_remote_copy(
            src_ref=source, dst_ref=target, send_sem=seg_send.at[n], recv_sem=seg_recv.at[n],
            device_id={"seg": before}, device_id_type=MESH,
        )
        for n, (source, target) in enumerate([(site_right_hbm, site_right), (right_hbm, right)])
    ]
    for copy in seg_copies:
        copy.start()

    locals_[1].wait()
    def pick_left(k, carry):
        for t in range(terms):
            picked[t * blocks + k] = left[t, left_ids[k]] * (sources[t, k] >= 0).astype(F32)
        return carry

    lax.fori_loop(0, blocks, pick_left, 0)

    def split_left(n, carry):
        high, low = split(picked[n])
        left_split[n, :tile] = high
        left_split[n, tile:] = low
        return carry

    lax.fori_loop(0, terms * blocks, split_left, 0)
    locals_[2].wait()
    for k in range(blocks):
        inverse[k * tile:(k + 1) * tile] = 1.0 / precond[k:k + 1, :].reshape(tile, tile)
    vector[...] = jnp.zeros_like(vector)
    image[...] = jnp.zeros_like(image)

    zero = jnp.zeros((8, tile), F32)

    def at(k):
        return pl.ds(pl.multiple_of(k * tile, tile), tile)

    def store_search(length):
        def block(k, carry):
            value = search[at(k)] * length
            search[at(k)] = value
            high, low = split(value)
            search_high[k] = high
            search_low[k] = low
            return carry

        lax.fori_loop(0, blocks, block, 0)

    locals_[0].wait()
    seg_copies[0].wait()
    def guess(k, total):
        a_high, a_low = split(site_left[k])
        b_high, b_low = split(site_right[k])
        value = dot(a_high, b_high) + (dot(a_high, b_low) + dot(a_low, b_high))
        search[at(k)] = value
        return total + folded(value * value)

    store_search(1.0 / jnp.sqrt(total_of(lax.fori_loop(0, blocks, guess, zero)) + EPSILON))

    seg_copies[1].wait()
    def pick_right(k, carry):
        for t in range(terms):
            picked[t * blocks + k] = right[t, right_ids[k]]
        return carry

    lax.fori_loop(0, blocks, pick_right, 0)

    def split_right(k, carry):
        for t in range(terms):
            high, low = split(picked[t * blocks + k].T)
            right_high[k, t * tile:(t + 1) * tile] = high
            right_low[k, t * tile:(t + 1) * tile] = low
        return carry

    lax.fori_loop(0, blocks, split_right, 0)

    def apply_local():
        def pick(k, carry):
            for t in range(terms):
                source = jnp.maximum(sources[t, k], 0)
                feed_high[t * blocks + k] = search_high[source]
                feed_low[t * blocks + k] = search_low[source]
            return carry

        lax.fori_loop(0, blocks, pick, 0)

        def block(k, carry):
            highs, lows = [], []
            for t in range(terms):
                held = t * blocks + k
                both = dot(left_split[held], feed_high[held])
                inner = both[:tile] + (both[tile:] + dot(left_split[held, :tile], feed_low[held]))
                high, low = split(inner)
                highs.append(high)
                lows.append(low)
            high = jnp.concatenate(highs, axis=1)
            both = dot(jnp.concatenate([high, jnp.concatenate(lows, axis=1)], axis=0), right_high[k])
            part[at(k)] = both[:tile] + (both[tile:] + dot(high, right_low[k]))
            return carry

        lax.fori_loop(0, blocks, block, 0)

    def to_partner(n, distance):
        owner = peer(distance) * 2 + 1 - column
        return pltpu.make_async_remote_copy(
            src_ref=part.at[rows(owner)], dst_ref=pair_in.at[n], send_sem=pair_send.at[n],
            recv_sem=pair_recv.at[n], device_id={"term": partner}, device_id_type=MESH,
        )

    def along_line(distance):
        return pltpu.make_async_remote_copy(
            src_ref=line_out.at[distance], dst_ref=line_in.at[distance], send_sem=line_send.at[distance],
            recv_sem=line_recv.at[distance], device_id={"term": peer(distance) * 2 + column},
            device_id_type=MESH,
        )

    def sum_out(distance):
        mine = rows(me)
        return pltpu.make_async_remote_copy(
            src_ref=search_image.at[mine], dst_ref=search_image.at[mine], send_sem=out_send.at[distance],
            recv_sem=out_recv.at[distance], device_id={"term": peer(distance) * 2 + column},
            device_id_type=MESH,
        )

    def sum_across(distance):
        held = rows(peer(places - distance) * 2 + column)
        return pltpu.make_async_remote_copy(
            src_ref=search_image.at[held], dst_ref=search_image.at[held], send_sem=across_send.at[distance],
            recv_sem=across_recv.at[distance], device_id={"term": partner}, device_id_type=MESH,
        )

    order = list(range(1, places)) + [0]

    def sum_terms():
        pairs = [to_partner(distance, distance) for distance in order]
        for copy in pairs:
            copy.start()
        lines = []
        for distance, copy in zip(order, pairs):
            copy.wait_recv()
            summed = pair_in[distance] + part[rows(peer(distance) * 2 + column)]
            if distance:
                line_out[distance] = summed
                lines.append(along_line(distance))
                lines[-1].start()
        for copy in lines:
            copy.wait_recv()
        for distance in range(1, places):
            summed = summed + line_in[distance]
        search_image[rows(me)] = summed
        outs = [sum_out(distance) for distance in range(1, places)]
        for copy in outs:
            copy.start()
        acrosses = [sum_across(distance) for distance in range(places)]
        acrosses[0].start()
        for distance in range(1, places):
            outs[distance - 1].wait_recv()
            acrosses[distance].start()
        for copy in acrosses:
            copy.wait_recv()
        for copy in pairs + lines + outs + acrosses:
            copy.wait_send()

    def step(iteration, energy):
        apply_local()
        sum_terms()
        first = iteration == 0
        def measures(k, sums):
            v, i, s, h = vector[at(k)], image[at(k)], search[at(k)], search_image[at(k)]
            return sums[0] + folded(v * h + s * i), sums[1] + folded(s * h)

        cross, own = lax.fori_loop(0, blocks, measures, (zero, zero))
        coupling, curvature = 0.5 * total_of(cross), total_of(own)
        half_gap = 0.5 * (energy - curvature)
        radius = jnp.sqrt(half_gap * half_gap + coupling * coupling)
        keep = jnp.where(
            half_gap >= 0, coupling * coupling / (radius + jnp.abs(half_gap)), radius - half_gap
        )
        norm = jnp.sqrt(keep * keep + coupling * coupling)
        keep, mix = jnp.where(first, 0.0, keep / norm), jnp.where(first, 1.0, -coupling / norm)
        def update(k, total):
            new_vector = keep * vector[at(k)] + mix * search[at(k)]
            new_image = keep * image[at(k)] + mix * search_image[at(k)]
            vector[at(k)] = new_vector
            image[at(k)] = new_image
            return total + folded(new_vector * new_image)

        energy = total_of(lax.fori_loop(0, blocks, update, zero))

        def scale_residual(k, total):
            scaled = (image[at(k)] - energy * vector[at(k)]) * inverse[at(k)]
            search[at(k)] = scaled
            return total + folded(vector[at(k)] * scaled)

        projection = total_of(lax.fori_loop(0, blocks, scale_residual, zero))

        def remove(k, total):
            remainder = search[at(k)] - projection * vector[at(k)]
            search[at(k)] = remainder
            return total + folded(remainder * remainder)

        store_search(1.0 / jnp.sqrt(total_of(lax.fori_loop(0, blocks, remove, zero)) + EPSILON))
        return energy

    energy = lax.fori_loop(0, ITERS + 1, step, jnp.zeros((1, 1), F32))
    energy_ref[...] = jnp.broadcast_to(energy, energy_ref.shape)
    scale = math.sqrt(blocks * tile * tile)
    for k in range(blocks):
        if share % 8 == 0:
            out_ref[k] = vector[pl.ds(pl.multiple_of(k * tile + me * share, 8), share)] * scale
        else:
            out_ref[k] = vector[k * tile:(k + 1) * tile] * scale


def shards(
    devices, segs,
    envs_left, envs_right, site_left, site_right, precondition, source_block, left_tile, right_tile,
):
    terms, tiles, tile = envs_left.shape[1], envs_left.shape[2], envs_left.shape[3]
    blocks = site_left.shape[1]
    piece = blocks * tile // devices
    places = devices // 2
    share = tile // devices
    out_rows = share if share % 8 == 0 else tile
    flat = pltpu.VMEM((blocks * tile, tile), F32)
    stack = pltpu.VMEM((blocks, tile, tile), F32)
    slots = pltpu.VMEM((places, piece, tile), F32)
    sems = pltpu.SemaphoreType.DMA((places,))
    hbm = pl.BlockSpec(memory_space=pl.ANY)
    smem = pl.BlockSpec(memory_space=pltpu.SMEM)
    vmem = pl.BlockSpec(memory_space=pltpu.VMEM)
    out, energy = pl.pallas_call(
        functools.partial(kernel, devices, segs, blocks, tile, terms, share),
        out_shape=(
            jax.ShapeDtypeStruct((blocks, out_rows, tile), F32),
            jax.ShapeDtypeStruct((8, 128), F32),
        ),
        in_specs=[hbm] * 5 + [smem] * 3,
        out_specs=(vmem, vmem),
        scratch_shapes=[
            pltpu.VMEM((terms, tiles, tile, tile), F32),
            pltpu.VMEM((terms, tiles, tile, tile), F32),
            stack,
            stack,
            pltpu.VMEM((blocks, tile * tile), F32),
            pltpu.VMEM((terms * blocks, 2 * tile, tile), BF16),
            pltpu.VMEM((blocks, terms * tile, tile), BF16),
            pltpu.VMEM((blocks, terms * tile, tile), BF16),
            pltpu.VMEM((blocks, tile, tile), BF16),
            pltpu.VMEM((blocks, tile, tile), BF16),
            pltpu.VMEM((terms * blocks, tile, tile), F32),
            pltpu.VMEM((terms * blocks, tile, tile), BF16),
            pltpu.VMEM((terms * blocks, tile, tile), BF16),
            flat, flat, flat, flat, flat, flat,
            slots, slots, slots,
            pltpu.SemaphoreType.DMA((3,)),
            pltpu.SemaphoreType.DMA((2,)),
            pltpu.SemaphoreType.DMA((2,)),
            sems, sems, sems, sems, sems, sems, sems, sems,
        ],
        compiler_params=pltpu.CompilerParams(
            collective_id=0, has_side_effects=True, vmem_limit_bytes=40 * 1024 * 1024
        ),
    )(
        envs_left[0], envs_right[0], site_left[0], site_right[0], precondition[0],
        source_block[0], left_tile[0], right_tile[0],
    )
    if out_rows != share:
        out = lax.dynamic_slice_in_dim(out, lax.axis_index("term") * share, share, 1)
    return (out.reshape(1, blocks, share * tile), energy[0, :1])


def solution(mesh):
    in_specs = (
        P("seg", "term", None, None, None),
        P("seg", "term", None, None, None),
        P("seg", None, None, None),
        P("seg", None, None, None),
        P("seg", None, None),
        P("seg", "term", None),
        P("seg", None),
        P("seg", None),
    )
    out_specs = (P("seg", None, "term"), P("seg"))
    body = functools.partial(shards, mesh.shape["term"], mesh.shape["seg"])
    return jax.shard_map(body, mesh=mesh, in_specs=in_specs, out_specs=out_specs, check_vma=False)
```

time: 487 us -> 136 us (0.28)
  waiting for transfers between devices: 368 us -> 0 us
  Pallas kernels: 0 us -> 129 us
  other arithmetic: 45.3 us -> 0 us
  between operations: 28.7 us -> 0.71 us
  matrix products: 18 us -> 0 us
  local copies, waits for them, and re-layouts: 22.5 us -> 5.54 us
    psum x5 -> x0, waiting for transfers between devices: 361 us -> none  [apply_whole(): return lax.psum(apply_local(full_vector), 'term')]
    pallas_call x0 -> x1, Pallas kernels: none -> 129 us  [shards(): pl.pallas_call(functools.partial(kernel, devices, segs, blocks, tile, ter...]
    reduce_sum x17 -> x0, other arithmetic: 33.5 us -> none  [the longest x5 9.4 us: shards(): energy = jnp.sum(vector * image)]
    dot_general x11 -> x0, matrix products: 18 us -> none  [the longest x5 11.3 us: local_terms(): jnp.einsum('tkab,tkbc->tkac', left_chosen, pieces, precision=FINEST)]
    div x5 -> x0, other arithmetic: 11 us -> none  [the longest x4 11 us: shards(): search = remainder / jnp.sqrt(jnp.sum(remainder * remainder) + EPSILON)]
    gather x7 -> x0, local copies, waits for them, and re-layouts: 10.9 us -> none  [the longest x5 8.46 us: local_terms(): pieces = tile_stack[safe_sources] * active_mask]
    ppermute x2 -> x0, waiting for transfers between devices: 6.98 us -> none  [passed_along(): return lax.ppermute(value, axis, pairs)]
    unnamed x51 -> x16, local copies, waits for them, and re-layouts: 10.9 us -> 5.02 us
  transfers between devices with their start and end apart: 7 -> 0, of which waited for: 7 -> 0; matrix products, arithmetic and copies ran while one was open for 1% -> 0% of each run, Pallas kernels for 0% -> 0%
where the time goes in v1:
time: 136 us
  Pallas kernels  129 us (95%)
  local copies, waits for them, and re-layouts  5.54 us (4%)
    pallas_call x1, Pallas kernels, shards(): pl.pallas_call(functools.partial(kernel, devices, segs, blocks, tile, ter...  129 us
    unnamed x16, local copies, waits for them, and re-layouts  5.02 us

profile of v1, /device:TPU:0, one launch (start us, length us, event | category | flops | bytes accessed | tf_op | source)
XLA Modules:
  0.0 135.7 jit_solution(12654681124586414972)
XLA Ops:
  0.6 0.0 copy-start.2
  0.6 0.0 copy-start.3
  0.7 0.0 copy-start.6
  0.7 1.3 copy.14
  2.0 0.0 copy-start.4
  2.0 0.0 copy-start.5
  2.0 0.0 copy-done.2
  2.0 0.0 copy-done.3
  2.0 0.0 copy-done.6
  2.0 0.6 copy-done.4
  2.6 0.0 copy-done.5
  2.7 0.0 copy-start
  2.7 1.2 copy-done
  3.9 0.0 copy-start.1
  3.9 1.2 copy-done.1
  5.1 129.5 %shard_map.95 = (f32[6,16,128]{2,1,0:T(8,128)S(1)}, f32[8,128]{1,0:T(8,128)S(1)}) custom-call(f32[2,8,128,128]{3,2,1,0:T(8,128)S(1)} %bitcast.13, f32[2,8,128,128]{3,2,1,0:T(8,128)S(1)} %bitcast.14, f32[6,128,128]{2,1,0:T(8,128)S(1)} %bitcast.15, f32[6,128,128]{2,1,0:T(8,128)S(1)} %bitcast.16, f32[6,16384]{1,0:T(8,128)S(1)} %bitcast.12, ...), custom_call_target="tpu_custom_call" | custom-call | tf_op jit(solution)/shard_map/pallas_call | solution.py:308
  134.6 0.5 slice.3
  135.1 0.6 copy.16
Async XLA Ops:
  0.6 1.4 %copy-start.2 = (f32[1,6,128,128]{3,2,1,0:T(8,128)S(1)}, f32[1,6,128,128]{3,2,1,0:T(8,128)}, u32[]{:S(2)}) copy-start(f32[1,6,128,128]{3,2,1,0:T(8,128)} %param.10) | copy-start | bytes 1179652
  0.6 1.4 %copy-start.3 = (f32[1,6,128,128]{3,2,1,0:T(8,128)S(1)}, f32[1,6,128,128]{3,2,1,0:T(8,128)}, u32[]{:S(2)}) copy-start(f32[1,6,128,128]{3,2,1,0:T(8,128)} %param.11) | copy-start | bytes 1179652
  0.7 1.4 %copy-start.6 = (s32[1,6]{1,0:T(1,128)S(1)}, s32[1,6]{1,0:T(1,128)}, u32[]{:S(2)}) copy-start(s32[1,6]{1,0:T(1,128)} %param.15) | copy-start | bytes 76
  2.0 0.7 copy-start.4
  2.0 0.7 copy-start.5
  2.7 1.2 copy-start
  3.9 1.2 copy-start.1

commit v2 on v1

--- a/solution.py
+++ b/solution.py
@@ -9,6 +9,7 @@
 from jax.sharding import PartitionSpec as P
 
 ITERS = 4
+PARTS = (3, 2, 1)
 EPSILON = 1e-06
 MESH = pl.DeviceIdType.MESH
 F32 = jnp.float32
@@ -34,7 +35,7 @@
 
 
 def kernel(
-    devices, segs, blocks, tile, terms, share,
+    devices, segs, blocks, tile, terms, share, parts,
     left_hbm, right_hbm, site_left_hbm, site_right_hbm, precond_hbm, sources, left_ids, right_ids,
     out_ref, energy_ref,
     left, right, site_left, site_right, precond, left_split, right_high, right_low,
@@ -48,10 +49,10 @@
     places = devices // 2
     partner = place * 2 + 1 - column
     before, after = (seg + segs - 1) % segs, (seg + 1) % segs
-    piece = blocks * tile // devices
-
-    def rows(owner):
-        return pl.ds(pl.multiple_of(owner * piece, 8), piece)
+    piece = blocks * tile // (parts * devices)
+
+    def rows(part_id, owner):
+        return pl.ds(pl.multiple_of((part_id * devices + owner) * piece, 8), piece)
 
     def peer(distance):
         return (place + distance) % places
@@ -80,10 +81,47 @@
             src_ref=source, dst_ref=target, send_sem=seg_send.at[n], recv_sem=seg_recv.at[n],
             device_id={"seg": before}, device_id_type=MESH,
         )
-        for n, (source, target) in enumerate([(site_right_hbm, site_right), (right_hbm, right)])
+        for n, (source, target) in enumerate(
+            [(site_right_hbm.at[rows(h, me)], site_right.at[rows(h, me)]) for h in range(parts)]
+            + [(right_hbm, right)]
+        )
     ]
     for copy in seg_copies:
         copy.start()
+
+    def send_out(buffer, h, distance):
+        mine = rows(h, me)
+        return pltpu.make_async_remote_copy(
+            src_ref=buffer.at[mine], dst_ref=buffer.at[mine], send_sem=out_send.at[h * places + distance],
+            recv_sem=out_recv.at[h * places + distance],
+            device_id={"term": peer(distance) * 2 + column}, device_id_type=MESH,
+        )
+
+    def send_across(buffer, h, distance):
+        held = rows(h, peer(places - distance) * 2 + column)
+        return pltpu.make_async_remote_copy(
+            src_ref=buffer.at[held], dst_ref=buffer.at[held], send_sem=across_send.at[h * places + distance],
+            recv_sem=across_recv.at[h * places + distance], device_id={"term": partner}, device_id_type=MESH,
+        )
+
+    def spread(buffer, ready):
+        outs, acrosses = [], []
+        for h in range(parts):
+            ready(h)
+            outs.append([send_out(buffer, h, distance) for distance in range(1, places)])
+            acrosses.append([send_across(buffer, h, distance) for distance in range(places)])
+            for copy in outs[h] + acrosses[h][:1]:
+                copy.start()
+        for h in range(parts):
+            for distance in range(1, places):
+                outs[h][distance - 1].wait_recv()
+                acrosses[h][distance].start()
+        for h in range(parts):
+            for copy in acrosses[h]:
+                copy.wait_recv()
+        for h in range(parts):
+            for copy in outs[h] + acrosses[h]:
+                copy.wait_send()
 
     locals_[1].wait()
     def pick_left(k, carry):
@@ -123,17 +161,17 @@
         lax.fori_loop(0, blocks, block, 0)
 
     locals_[0].wait()
-    seg_copies[0].wait()
+    spread(site_right, lambda h: seg_copies[h].wait())
     def guess(k, total):
         a_high, a_low = split(site_left[k])
-        b_high, b_low = split(site_right[k])
+        b_high, b_low = split(site_right[at(k)])
         value = dot(a_high, b_high) + (dot(a_high, b_low) + dot(a_low, b_high))
         search[at(k)] = value
         return total + folded(value * value)
 
     store_search(1.0 / jnp.sqrt(total_of(lax.fori_loop(0, blocks, guess, zero)) + EPSILON))
 
-    seg_copies[1].wait()
+    seg_copies[parts].wait()
     def pick_right(k, carry):
         for t in range(terms):
             picked[t * blocks + k] = right[t, right_ids[k]]
@@ -150,7 +188,7 @@
 
     lax.fori_loop(0, blocks, split_right, 0)
 
-    def apply_local():
+    def apply_local(low_block, high_block):
         def pick(k, carry):
             for t in range(terms):
                 source = jnp.maximum(sources[t, k], 0)
@@ -158,7 +196,7 @@
                 feed_low[t * blocks + k] = search_low[source]
             return carry
 
-        lax.fori_loop(0, blocks, pick, 0)
+        lax.fori_loop(low_block, high_block, pick, 0)
 
         def block(k, carry):
             highs, lows = [], []
@@ -174,72 +212,58 @@
             part[at(k)] = both[:tile] + (both[tile:] + dot(high, right_low[k]))
             return carry
 
-        lax.fori_loop(0, blocks, block, 0)
-
-    def to_partner(n, distance):
-        owner = peer(distance) * 2 + 1 - column
+        lax.fori_loop(low_block, high_block, block, 0)
+
+    def to_partner(h, distance):
+        slot = h * places + distance
         return pltpu.make_async_remote_copy(
-            src_ref=part.at[rows(owner)], dst_ref=pair_in.at[n], send_sem=pair_send.at[n],
-            recv_sem=pair_recv.at[n], device_id={"term": partner}, device_id_type=MESH,
-        )
-
-    def along_line(distance):
+            src_ref=part.at[rows(h, peer(distance) * 2 + 1 - column)], dst_ref=pair_in.at[slot],
+            send_sem=pair_send.at[slot], recv_sem=pair_recv.at[slot],
+            device_id={"term": partner}, device_id_type=MESH,
+        )
+
+    def along_line(h, distance):
+        slot = h * places + distance
         return pltpu.make_async_remote_copy(
-            src_ref=line_out.at[distance], dst_ref=line_in.at[distance], send_sem=line_send.at[distance],
-            recv_sem=line_recv.at[distance], device_id={"term": peer(distance) * 2 + column},
+            src_ref=line_out.at[slot], dst_ref=line_in.at[slot], send_sem=line_send.at[slot],
+            recv_sem=line_recv.at[slot], device_id={"term": peer(distance) * 2 + column},
             device_id_type=MESH,
         )
 
-    def sum_out(distance):
-        mine = rows(me)
-        return pltpu.make_async_remote_copy(
-            src_ref=search_image.at[mine], dst_ref=search_image.at[mine], send_sem=out_send.at[distance],
-            recv_sem=out_recv.at[distance], device_id={"term": peer(distance) * 2 + column},
-            device_id_type=MESH,
-        )
-
-    def sum_across(distance):
-        held = rows(peer(places - distance) * 2 + column)
-        return pltpu.make_async_remote_copy(
-            src_ref=search_image.at[held], dst_ref=search_image.at[held], send_sem=across_send.at[distance],
-            recv_sem=across_recv.at[distance], device_id={"term": partner}, device_id_type=MESH,
-        )
-
     order = list(range(1, places)) + [0]
 
-    def sum_terms():
-        pairs = [to_partner(distance, distance) for distance in order]
-        for copy in pairs:
-            copy.start()
-        lines = []
-        for distance, copy in zip(order, pairs):
-            copy.wait_recv()
-            summed = pair_in[distance] + part[rows(peer(distance) * 2 + column)]
-            if distance:
-                line_out[distance] = summed
-                lines.append(along_line(distance))
-                lines[-1].start()
-        for copy in lines:
-            copy.wait_recv()
-        for distance in range(1, places):
-            summed = summed + line_in[distance]
-        search_image[rows(me)] = summed
-        outs = [sum_out(distance) for distance in range(1, places)]
-        for copy in outs:
-            copy.start()
-        acrosses = [sum_across(distance) for distance in range(places)]
-        acrosses[0].start()
-        for distance in range(1, places):
-            outs[distance - 1].wait_recv()
-            acrosses[distance].start()
-        for copy in acrosses:
-            copy.wait_recv()
-        for copy in pairs + lines + outs + acrosses:
-            copy.wait_send()
+    def apply():
+        pairs, lines = [], []
+        for h in range(parts):
+            apply_local(h * blocks // parts, (h + 1) * blocks // parts)
+            pairs.append([to_partner(h, distance) for distance in order])
+            for copy in pairs[h]:
+                copy.start()
+        for h in range(parts):
+            lines.append([])
+            for distance, copy in zip(order, pairs[h]):
+                copy.wait_recv()
+                slot = h * places + distance
+                line_out[slot] = pair_in[slot] + part[rows(h, peer(distance) * 2 + column)]
+                if distance:
+                    lines[h].append(along_line(h, distance))
+                    lines[h][-1].start()
+
+        def finish(h):
+            for copy in lines[h]:
+                copy.wait_recv()
+            summed = line_out[h * places]
+            for distance in range(1, places):
+                summed = summed + line_in[h * places + distance]
+            search_image[rows(h, me)] = summed
+
+        spread(search_image, finish)
+        for h in range(parts):
+            for copy in pairs[h] + lines[h]:
+                copy.wait_send()
 
     def step(iteration, energy):
-        apply_local()
-        sum_terms()
+        apply()
         first = iteration == 0
         def measures(k, sums):
             v, i, s, h = vector[at(k)], image[at(k)], search[at(k)], search_image[at(k)]
@@ -295,18 +319,19 @@
     terms, tiles, tile = envs_left.shape[1], envs_left.shape[2], envs_left.shape[3]
     blocks = site_left.shape[1]
     piece = blocks * tile // devices
+    parts = next(n for n in PARTS if blocks % n == 0 and piece % (8 * n) == 0)
     places = devices // 2
     share = tile // devices
     out_rows = share if share % 8 == 0 else tile
     flat = pltpu.VMEM((blocks * tile, tile), F32)
     stack = pltpu.VMEM((blocks, tile, tile), F32)
-    slots = pltpu.VMEM((places, piece, tile), F32)
-    sems = pltpu.SemaphoreType.DMA((places,))
+    slots = pltpu.VMEM((parts * places, piece // parts, tile), F32)
+    sems = pltpu.SemaphoreType.DMA((parts * places,))
     hbm = pl.BlockSpec(memory_space=pl.ANY)
     smem = pl.BlockSpec(memory_space=pltpu.SMEM)
     vmem = pl.BlockSpec(memory_space=pltpu.VMEM)
     out, energy = pl.pallas_call(
-        functools.partial(kernel, devices, segs, blocks, tile, terms, share),
+        functools.partial(kernel, devices, segs, blocks, tile, terms, share, parts),
         out_shape=(
             jax.ShapeDtypeStruct((blocks, out_rows, tile), F32),
             jax.ShapeDtypeStruct((8, 128), F32),
@@ -317,7 +342,7 @@
             pltpu.VMEM((terms, tiles, tile, tile), F32),
             pltpu.VMEM((terms, tiles, tile, tile), F32),
             stack,
-            stack,
+            flat,
             pltpu.VMEM((blocks, tile * tile), F32),
             pltpu.VMEM((terms * blocks, 2 * tile, tile), BF16),
             pltpu.VMEM((blocks, terms * tile, tile), BF16),
@@ -330,15 +355,15 @@
             flat, flat, flat, flat, flat, flat,
             slots, slots, slots,
             pltpu.SemaphoreType.DMA((3,)),
-            pltpu.SemaphoreType.DMA((2,)),
-            pltpu.SemaphoreType.DMA((2,)),
+            pltpu.SemaphoreType.DMA((parts + 1,)),
+            pltpu.SemaphoreType.DMA((parts + 1,)),
             sems, sems, sems, sems, sems, sems, sems, sems,
         ],
         compiler_params=pltpu.CompilerParams(
             collective_id=0, has_side_effects=True, vmem_limit_bytes=40 * 1024 * 1024
         ),
     )(
-        envs_left[0], envs_right[0], site_left[0], site_right[0], precondition[0],
+        envs_left[0], envs_right[0], site_left[0], site_right[0].reshape(blocks * tile, tile), precondition[0],
         source_block[0], left_tile[0], right_tile[0],
     )
     if out_rows != share:

time: 136 us -> 118 us (0.87)
  Pallas kernels: 129 us -> 111 us
    pallas_call x1, Pallas kernels: 129 us -> 111 us  [shards(): pl.pallas_call(functools.partial(kernel, devices, segs, blocks, tile, ter...]
where the time goes in v2:
time: 118 us
  Pallas kernels  111 us (94%)
  local copies, waits for them, and re-layouts  5.54 us (5%)
    pallas_call x1, Pallas kernels, shards(): pl.pallas_call(functools.partial(kernel, devices, segs, blocks, tile, ter...  111 us
    unnamed x16, local copies, waits for them, and re-layouts  5.02 us

profile of v2, /device:TPU:0, one launch (start us, length us, event | category | flops | bytes accessed | tf_op | source)
XLA Modules:
  0.0 117.7 jit_solution(2504794386153460517)
XLA Ops:
  0.6 0.0 copy-start.2
  0.6 0.0 copy-start.3
  0.7 0.0 copy-start.6
  0.7 1.3 %copy.14 = f32[1,6,16384]{2,1,0:T(8,128)S(1)} copy(f32[1,6,16384]{2,0,1:T(1,128)} %param.12) | data formatting | bytes 786432
  2.0 0.0 copy-start.4
  2.0 0.0 copy-start.5
  2.0 0.0 copy-done.2
  2.0 0.0 copy-done.3
  2.0 0.0 copy-done.6
  2.0 0.6 copy-done.4
  2.6 0.0 copy-done.5
  2.7 0.0 copy-start
  2.7 1.2 %copy-done = f32[1,2,8,128,128]{4,3,2,1,0:T(8,128)S(1)} copy-done((f32[1,2,8,128,128]{4,3,2,1,0:T(8,128)S(1)}, f32[1,2,8,128,128]{4,3,2,1,0:T(8,128)}, u32[]{:S(2)}) %copy-start) | copy-done | bytes 1048600
  3.9 0.0 copy-start.1
  3.9 1.2 %copy-done.1 = f32[1,2,8,128,128]{4,3,2,1,0:T(8,128)S(1)} copy-done((f32[1,2,8,128,128]{4,3,2,1,0:T(8,128)S(1)}, f32[1,2,8,128,128]{4,3,2,1,0:T(8,128)}, u32[]{:S(2)}) %copy-start.1) | copy-done | bytes 1048600
  5.1 111.5 %shard_map.95 = (f32[6,16,128]{2,1,0:T(8,128)S(1)}, f32[8,128]{1,0:T(8,128)S(1)}) custom-call(f32[2,8,128,128]{3,2,1,0:T(8,128)S(1)} %bitcast.13, f32[2,8,128,128]{3,2,1,0:T(8,128)S(1)} %bitcast.14, f32[6,128,128]{2,1,0:T(8,128)S(1)} %bitcast.15, f32[768,128]{1,0:T(8,128)S(1)} %bitcast.16, f32[6,16384]{1,0:T(8,128)S(1)} %bitcast.12, s32[2,6]{1,0:T(2,128)S(1)} %bitcast.18, ...), custom_call_target="tpu_custom_call" | custom-call | tf_op jit(solution)/shard_map/pallas_call | solution.py:333
  116.6 0.5 slice.3
  117.1 0.6 copy.16
Async XLA Ops:
  0.6 1.4 %copy-start.2 = (f32[1,6,128,128]{3,2,1,0:T(8,128)S(1)}, f32[1,6,128,128]{3,2,1,0:T(8,128)}, u32[]{:S(2)}) copy-start(f32[1,6,128,128]{3,2,1,0:T(8,128)} %param.10) | copy-start | bytes 1179652
  0.6 1.4 %copy-start.3 = (f32[1,6,128,128]{3,2,1,0:T(8,128)S(1)}, f32[1,6,128,128]{3,2,1,0:T(8,128)}, u32[]{:S(2)}) copy-start(f32[1,6,128,128]{3,2,1,0:T(8,128)} %param.11) | copy-start | bytes 1179652
  0.7 1.4 %copy-start.6 = (s32[1,6]{1,0:T(1,128)S(1)}, s32[1,6]{1,0:T(1,128)}, u32[]{:S(2)}) copy-start(s32[1,6]{1,0:T(1,128)} %param.15) | copy-start | bytes 76
  2.0 0.7 copy-start.4
  2.0 0.7 copy-start.5
  2.7 1.2 %copy-start = (f32[1,2,8,128,128]{4,3,2,1,0:T(8,128)S(1)}, f32[1,2,8,128,128]{4,3,2,1,0:T(8,128)}, u32[]{:S(2)}) copy-start(f32[1,2,8,128,128]{4,3,2,1,0:T(8,128)} %param.8) | copy-start | bytes 3145732
  3.9 1.2 %copy-start.1 = (f32[1,2,8,128,128]{4,3,2,1,0:T(8,128)S(1)}, f32[1,2,8,128,128]{4,3,2,1,0:T(8,128)}, u32[]{:S(2)}) copy-start(f32[1,2,8,128,128]{4,3,2,1,0:T(8,128)} %param.9) | copy-start | bytes 3145732

commit v3 on v2

--- a/solution.py
+++ b/solution.py
@@ -9,7 +9,7 @@
 from jax.sharding import PartitionSpec as P
 
 ITERS = 4
-PARTS = (3, 2, 1)
+PARTS = (6, 3, 2, 1)
 EPSILON = 1e-06
 MESH = pl.DeviceIdType.MESH
 F32 = jnp.float32
@@ -54,6 +54,9 @@
     def rows(part_id, owner):
         return pl.ds(pl.multiple_of((part_id * devices + owner) * piece, 8), piece)
 
+    def at(k):
+        return pl.ds(pl.multiple_of(k * tile, tile), tile)
+
     def peer(distance):
         return (place + distance) % places
 
@@ -83,7 +86,7 @@
         )
         for n, (source, target) in enumerate(
             [(site_right_hbm.at[rows(h, me)], site_right.at[rows(h, me)]) for h in range(parts)]
-            + [(right_hbm, right)]
+            + [(right_hbm.at[t], right.at[t]) for t in range(terms)]
         )
     ]
     for copy in seg_copies:
@@ -140,14 +143,11 @@
     lax.fori_loop(0, terms * blocks, split_left, 0)
     locals_[2].wait()
     for k in range(blocks):
-        inverse[k * tile:(k + 1) * tile] = 1.0 / precond[k:k + 1, :].reshape(tile, tile)
+        inverse[at(k)] = 1.0 / precond[at(k)]
     vector[...] = jnp.zeros_like(vector)
     image[...] = jnp.zeros_like(image)
 
     zero = jnp.zeros((8, tile), F32)
-
-    def at(k):
-        return pl.ds(pl.multiple_of(k * tile, tile), tile)
 
     def store_search(length):
         def block(k, carry):
@@ -171,22 +171,23 @@
 
     store_search(1.0 / jnp.sqrt(total_of(lax.fori_loop(0, blocks, guess, zero)) + EPSILON))
 
-    seg_copies[parts].wait()
-    def pick_right(k, carry):
-        for t in range(terms):
-            picked[t * blocks + k] = right[t, right_ids[k]]
-        return carry
-
-    lax.fori_loop(0, blocks, pick_right, 0)
-
-    def split_right(k, carry):
-        for t in range(terms):
-            high, low = split(picked[t * blocks + k].T)
+    for t in range(terms):
+        seg_copies[parts + t].wait()
+    for t in range(terms):
+
+        def pick_right(k, carry):
+            picked[k] = right[t, right_ids[k]]
+            return carry
+
+        lax.fori_loop(0, blocks, pick_right, 0)
+
+        def split_right(k, carry):
+            high, low = split(picked[k].T)
             right_high[k, t * tile:(t + 1) * tile] = high
             right_low[k, t * tile:(t + 1) * tile] = low
-        return carry
-
-    lax.fori_loop(0, blocks, split_right, 0)
+            return carry
+
+        lax.fori_loop(0, blocks, split_right, 0)
 
     def apply_local(low_block, high_block):
         def pick(k, carry):
@@ -343,7 +344,7 @@
             pltpu.VMEM((terms, tiles, tile, tile), F32),
             stack,
             flat,
-            pltpu.VMEM((blocks, tile * tile), F32),
+            flat,
             pltpu.VMEM((terms * blocks, 2 * tile, tile), BF16),
             pltpu.VMEM((blocks, terms * tile, tile), BF16),
             pltpu.VMEM((blocks, terms * tile, tile), BF16),
@@ -355,15 +356,15 @@
             flat, flat, flat, flat, flat, flat,
             slots, slots, slots,
             pltpu.SemaphoreType.DMA((3,)),
-            pltpu.SemaphoreType.DMA((parts + 1,)),
-            pltpu.SemaphoreType.DMA((parts + 1,)),
+            pltpu.SemaphoreType.DMA((parts + terms,)),
+            pltpu.SemaphoreType.DMA((parts + terms,)),
             sems, sems, sems, sems, sems, sems, sems, sems,
         ],
         compiler_params=pltpu.CompilerParams(
-            collective_id=0, has_side_effects=True, vmem_limit_bytes=40 * 1024 * 1024
+            collective_id=0, has_side_effects=True
         ),
     )(
-        envs_left[0], envs_right[0], site_left[0], site_right[0].reshape(blocks * tile, tile), precondition[0],
+        envs_left[0], envs_right[0], site_left[0], site_right[0].reshape(blocks * tile, tile), precondition.reshape(blocks * tile, tile),
         source_block[0], left_tile[0], right_tile[0],
     )
     if out_rows != share:

time: 118 us -> 115 us (0.975)
  local copies, waits for them, and re-layouts: 5.54 us -> 2.61 us
    unnamed x16 -> x1, local copies, waits for them, and re-layouts: 5.02 us -> 1.42 us
where the time goes in v3:
time: 115 us
  Pallas kernels  111 us (97%)
  local copies, waits for them, and re-layouts  2.61 us (2%)
    pallas_call x1, Pallas kernels, shards(): pl.pallas_call(functools.partial(kernel, devices, segs, blocks, tile, ter...  111 us

profile of v3, /device:TPU:0, one launch (start us, length us, event | category | flops | bytes accessed | tf_op | source)
XLA Modules:
  0.0 114.6 jit_solution(14216625620781769309)
XLA Ops:
  0.6 111.3 %shard_map.95 = (f32[6,16,128]{2,1,0:T(8,128)}, f32[8,128]{1,0:T(8,128)}) custom-call(f32[2,8,128,128]{3,2,1,0:T(8,128)} %bitcast.10, f32[2,8,128,128]{3,2,1,0:T(8,128)} %bitcast.11, f32[6,128,128]{2,1,0:T(8,128)} %bitcast.12, f32[768,128]{1,0:T(8,128)} %bitcast.13, f32[768,128]{1,0:T(8,128)} %bitcast.14, s32[2,6]{1,0:T(2,128)} %bitcast.16, s32[6]{0:T(128)} %bitcast.17, ...), custom_call_target="tpu_custom_call" | custom-call | tf_op jit(solution)/shard_map/pallas_call | solution.py:334
  111.9 1.2 %slice.3 = f32[1,1]{1,0:T(1,128)} slice(f32[8,128]{1,0:T(8,128)} %get-tuple-element.5), slice={[0:1], [0:1]} | slice | bytes 8 | tf_op jit(solution)/shard_map/slice | solution.py:372
  113.1 1.4 %copy.13 = f32[1,6,2048]{2,0,1:T(1,128)} copy(f32[1,6,2048]{2,0,1:T(1,128)} %bitcast.15) | data formatting | bytes 98304

commit v4 on v3

--- a/solution.py
+++ b/solution.py
@@ -279,19 +279,16 @@
         )
         norm = jnp.sqrt(keep * keep + coupling * coupling)
         keep, mix = jnp.where(first, 0.0, keep / norm), jnp.where(first, 1.0, -coupling / norm)
-        def update(k, total):
+        energy = keep * keep * energy + 2.0 * keep * mix * coupling + mix * mix * curvature
+
+        def scale_residual(k, total):
             new_vector = keep * vector[at(k)] + mix * search[at(k)]
             new_image = keep * image[at(k)] + mix * search_image[at(k)]
             vector[at(k)] = new_vector
             image[at(k)] = new_image
-            return total + folded(new_vector * new_image)
-
-        energy = total_of(lax.fori_loop(0, blocks, update, zero))
-
-        def scale_residual(k, total):
-            scaled = (image[at(k)] - energy * vector[at(k)]) * inverse[at(k)]
+            scaled = (new_image - energy * new_vector) * inverse[at(k)]
             search[at(k)] = scaled
-            return total + folded(vector[at(k)] * scaled)
+            return total + folded(new_vector * scaled)
 
         projection = total_of(lax.fori_loop(0, blocks, scale_residual, zero))
 

time: 115 us -> 114 us (level)
    pallas_call x1, Pallas kernels: 111 us -> 110 us  [shards(): pl.pallas_call(functools.partial(kernel, devices, segs, blocks, tile, ter...]
where the time goes in v4:
time: 114 us; the launch traced here: 113 us
  Pallas kernels  110 us (96%)
  local copies, waits for them, and re-layouts  2.61 us (2%)
    pallas_call x1, Pallas kernels, shards(): pl.pallas_call(functools.partial(kernel, devices, segs, blocks, tile, ter...  110 us

profile of v4, /device:TPU:0, one launch (start us, length us, event | category | flops | bytes accessed | tf_op | source)
XLA Modules:
  0.0 113.4 jit_solution(15688249124107222697)
XLA Ops:
  0.6 110.1 %shard_map.95 = (f32[6,16,128]{2,1,0:T(8,128)}, f32[8,128]{1,0:T(8,128)}) custom-call(f32[2,8,128,128]{3,2,1,0:T(8,128)} %bitcast.10, f32[2,8,128,128]{3,2,1,0:T(8,128)} %bitcast.11, f32[6,128,128]{2,1,0:T(8,128)} %bitcast.12, f32[768,128]{1,0:T(8,128)} %bitcast.13, f32[768,128]{1,0:T(8,128)} %bitcast.14, s32[2,6]{1,0:T(2,128)} %bitcast.16, s32[6]{0:T(128)} %bitcast.17, ...), custom_call_target="tpu_custom_call" | custom-call | tf_op jit(solution)/shard_map/pallas_call | solution.py:331
  110.8 1.2 %slice.3 = f32[1,1]{1,0:T(1,128)} slice(f32[8,128]{1,0:T(8,128)} %get-tuple-element.5), slice={[0:1], [0:1]} | slice | bytes 8 | tf_op jit(solution)/shard_map/slice | solution.py:369
  112.0 1.4 %copy.13 = f32[1,6,2048]{2,0,1:T(1,128)} copy(f32[1,6,2048]{2,0,1:T(1,128)} %bitcast.15) | data formatting | bytes 98304
